TPU v7x, 256 devices: a whole 4x4x8 slice. The times are simulated.
256 devices in a mesh: src: 8 (over y, core), tgt: 32 (over x, z).
Axes of the slice: x: 4, y: 4, z: 8, core: 2. Of those that a mesh axis runs over, the one named last changes fastest.
Arguments:
- source: bfloat16 [16384, 128], P('src'), may hold values from -6 to 6
- target: bfloat16 [32768, 128], P('tgt'), may hold values from -5 to 5
- start_map: float32 [128, 128], replicated, may hold values from -1 to 1
- warm_potential: float32 [32768], P('tgt'), may hold values from -60 to 24
Outputs:
- row_potential: float32 [16384], P('src')
- col_potential: float32 [32768], P('tgt')
- new_map: float32 [128, 128], replicated
All inputs are finite; a program needn't handle non-finite values.
Results may differ from a plain program's by a relative error of at most 0.0078.
Values sent between devices are 32-bit elements; how exact they have to be, the bound alone decides.
A program may use at most 64 MiB of HBM per device.

v0:
```python
import math
import jax
import jax.numpy as jnp
from jax import lax
from jax.sharding import PartitionSpec as P

ROUNDS = 3
NEWTON = 10
EPS = 0.05


def row_partials(rotated, target, col_pot, score_scale):
    row_count = rotated.shape[0]
    block_rows = math.gcd(row_count, 512)
    blocks = rotated.reshape(row_count // block_rows, block_rows, rotated.shape[1])

    def row_one_block(row_block):
        scores = (
            jnp.einsum("rd,cd->rc", row_block, target, preferred_element_type=jnp.float32)
            * score_scale
            + col_pot[None, :]
        )
        peak_val = jnp.max(scores, axis=1)
        totals = jnp.sum(jnp.exp(scores - peak_val[:, None]), axis=1)
        return (peak_val, totals)

    peak_val, totals = lax.map(row_one_block, blocks)
    return (peak_val.reshape(row_count), totals.reshape(row_count))


def col_partials(rotated, target, row_pot, score_scale):
    row_count = rotated.shape[0]
    block_rows = math.gcd(row_count, 512)
    blocks = rotated.reshape(row_count // block_rows, block_rows, rotated.shape[1])
    pots = row_pot.reshape(row_count // block_rows, block_rows)

    def col_one_block(inputs):
        row_block, pot_block = inputs
        scores = (
            jnp.einsum("rd,cd->rc", row_block, target, preferred_element_type=jnp.float32)
            * score_scale
            + pot_block[:, None]
        )
        peak_val = jnp.max(scores, axis=0)
        totals = jnp.sum(jnp.exp(scores - peak_val[None, :]), axis=0)
        return (peak_val, totals)

    peaks, totals = lax.map(col_one_block, (blocks, pots))
    peak_val = jnp.max(peaks, axis=0)
    return (peak_val, jnp.sum(totals * jnp.exp(peaks - peak_val[None, :]), axis=0))


def across_targets(peak_val, totals):
    global_peak = lax.pmax(peak_val, "tgt")
    totals = lax.psum(totals * jnp.exp(peak_val - global_peak), "tgt")
    peak_val = global_peak
    return peak_val + jnp.log(totals)


def across_sources(peak_val, totals):
    global_peak = lax.pmax(peak_val, "src")
    totals = lax.psum(totals * jnp.exp(peak_val - global_peak), "src")
    peak_val = global_peak
    return peak_val + jnp.log(totals)


def polar(matrix):
    iterate = matrix / jnp.sqrt(jnp.sum(matrix * matrix) + 1e-06)
    for newton_index in range(NEWTON):
        gram_matrix = jnp.dot(iterate.T, iterate, precision=lax.Precision.HIGHEST)
        iterate = 1.5 * iterate - 0.5 * jnp.dot(
            iterate, gram_matrix, precision=lax.Precision.HIGHEST
        )
    return iterate


def shards(source, target, start_map, warm_potential):
    width = source.shape[1]
    score_scale = 1.0 / (math.sqrt(width) * EPS)
    rows_all = source.shape[0] * lax.axis_size("src")
    cols_all = target.shape[0] * lax.axis_size("tgt")
    rotated = jnp.dot(
        source, start_map.astype(jnp.bfloat16), preferred_element_type=jnp.float32
    ).astype(jnp.bfloat16)
    col_pot = warm_potential
    for round_index in range(ROUNDS):
        row_pot = -math.log(rows_all) - across_targets(
            *row_partials(rotated, target, col_pot, score_scale)
        )
        col_pot = -math.log(cols_all) - across_sources(
            *col_partials(rotated, target, row_pot, score_scale)
        )
    row_lse = across_targets(*row_partials(rotated, target, col_pot, score_scale))
    row_pot = -math.log(rows_all) - row_lse
    rows_here = source.shape[0] // lax.axis_size("tgt")
    block_rows = math.gcd(rows_here * lax.axis_size("tgt"), 512)
    nblocks = rows_here * lax.axis_size("tgt") // block_rows

    def numerator_one_block(inputs):
        row_block, lse_block = inputs
        scores = (
            jnp.einsum("rd,cd->rc", row_block, target, preferred_element_type=jnp.float32)
            * score_scale
            + col_pot[None, :]
            - lse_block[:, None]
        )
        weights = jnp.exp(scores).astype(jnp.bfloat16)
        return jnp.dot(weights, target, preferred_element_type=jnp.float32)

    parts_out = lax.map(
        numerator_one_block,
        (rotated.reshape(nblocks, block_rows, width), row_lse.reshape(nblocks, block_rows)),
    )
    my_targets = lax.psum_scatter(
        parts_out.reshape(rows_here * lax.axis_size("tgt"), width),
        "tgt",
        scatter_dimension=0,
        tiled=True,
    )
    source_rows = lax.dynamic_slice_in_dim(source, lax.axis_index("tgt") * rows_here, rows_here, 0)
    partial_value = jnp.einsum(
        "rd,re->de", source_rows.astype(jnp.float32), my_targets, precision=lax.Precision.HIGHEST
    )
    covariance_sum = lax.psum(partial_value, ("src", "tgt"))
    new_map = polar(covariance_sum)
    return (EPS * row_pot, EPS * col_pot, new_map)


def solution(mesh):
    placed = (P("src", None), P("tgt", None), P(), P("tgt"))
    return jax.shard_map(
        shards, mesh=mesh, in_specs=placed, out_specs=(P("src"), P("tgt"), P()), check_vma=False
    )
```

profile of v0, /device:TPU:1, one launch (start us, length us, event | category | flops | bytes accessed | tf_op | source)
XLA Modules:
  0.0 1202.2 jit_solution(3626454813866031106)
XLA Ops:
  9.4 8.7 while.94
  9.4 1.5 fusion.139
  11.6 1.5 fusion.139
  13.7 1.5 fusion.139
  15.9 1.5 fusion.139
  18.1 65.3 %pmax.49 = f32[2048]{0:T(1024)S(1)} all-reduce(f32[2048]{0:T(1024)S(1)} %bitcast.221), channel_id=1, replica_groups=mesh['src'=8,'tgt'=32] {'tgt'}, use_global_device_ids=true, to_apply=%region_4.5 | all-reduce | flops 2048 | bytes 16384 | tf_op jit(solution)/shard_map/pmax | solution.py:54
  83.4 56.8 %psum.56 = f32[2048]{0:T(1024)S(1)} all-reduce(f32[2048]{0:T(1024)S(1)} %exponential_multiply_fusion.3), channel_id=1, replica_groups=mesh['src'=8,'tgt'=32] {'tgt'}, use_global_device_ids=true, to_apply=%region_5.6 | all-reduce | flops 2048 | bytes 16384 | tf_op jit(solution)/shard_map/psum | solution.py:55
  140.3 8.4 while.95
  146.6 1.4 fusion.141
  148.7 40.6 %pmax.50 = f32[1024]{0:T(1024)S(1)} all-reduce(f32[1024]{0:T(1024)S(1)} %reduce_max.90), channel_id=1, replica_groups=mesh['src'=8,'tgt'=32] {'src'}, use_global_device_ids=true, to_apply=%region_11.12 | all-reduce | flops 1024 | bytes 8192 | tf_op jit(solution)/shard_map/pmax | solution.py:61
  189.4 12.3 %psum.57 = f32[1024]{0:T(1024)S(1)} all-reduce(f32[1024]{0:T(1024)S(1)} %exponential_multiply_fusion.6), channel_id=1, replica_groups=mesh['src'=8,'tgt'=32] {'src'}, use_global_device_ids=true, to_apply=%region_13.14 | all-reduce | flops 1024 | bytes 8192 | tf_op jit(solution)/shard_map/psum | solution.py:62
  201.7 8.7 while.96
  201.7 1.5 fusion.143
  203.9 1.5 fusion.143
  206.1 1.5 fusion.143
  208.2 1.5 fusion.143
  210.4 58.5 %pmax.51 = f32[2048]{0:T(1024)S(1)} all-reduce(f32[2048]{0:T(1024)S(1)} %bitcast.223), channel_id=1, replica_groups=mesh['src'=8,'tgt'=32] {'tgt'}, use_global_device_ids=true, to_apply=%region_18.19 | all-reduce | flops 2048 | bytes 16384 | tf_op jit(solution)/shard_map/pmax | solution.py:54
  268.9 56.8 %psum.58 = f32[2048]{0:T(1024)S(1)} all-reduce(f32[2048]{0:T(1024)S(1)} %exponential_multiply_fusion.2), channel_id=1, replica_groups=mesh['src'=8,'tgt'=32] {'tgt'}, use_global_device_ids=true, to_apply=%region_19.20 | all-reduce | flops 2048 | bytes 16384 | tf_op jit(solution)/shard_map/psum | solution.py:55
  325.8 8.4 while.97
  332.1 1.4 fusion.145
  334.2 40.5 %pmax.52 = f32[1024]{0:T(1024)S(1)} all-reduce(f32[1024]{0:T(1024)S(1)} %reduce_max.91), channel_id=1, replica_groups=mesh['src'=8,'tgt'=32] {'src'}, use_global_device_ids=true, to_apply=%region_25.26 | all-reduce | flops 1024 | bytes 8192 | tf_op jit(solution)/shard_map/pmax | solution.py:61
  374.8 12.4 %psum.59 = f32[1024]{0:T(1024)S(1)} all-reduce(f32[1024]{0:T(1024)S(1)} %exponential_multiply_fusion.5), channel_id=1, replica_groups=mesh['src'=8,'tgt'=32] {'src'}, use_global_device_ids=true, to_apply=%region_27.28 | all-reduce | flops 1024 | bytes 8192 | tf_op jit(solution)/shard_map/psum | solution.py:62
  387.2 8.7 while.98
  387.2 1.5 fusion.147
  389.4 1.5 fusion.147
  391.6 1.5 fusion.147
  393.8 1.5 fusion.147
  395.9 59.2 %pmax.53 = f32[2048]{0:T(1024)S(1)} all-reduce(f32[2048]{0:T(1024)S(1)} %bitcast.225), channel_id=1, replica_groups=mesh['src'=8,'tgt'=32] {'tgt'}, use_global_device_ids=true, to_apply=%region_32.33 | all-reduce | flops 2048 | bytes 16384 | tf_op jit(solution)/shard_map/pmax | solution.py:54
  455.1 57.0 %psum.60 = f32[2048]{0:T(1024)S(1)} all-reduce(f32[2048]{0:T(1024)S(1)} %exponential_multiply_fusion.1), channel_id=1, replica_groups=mesh['src'=8,'tgt'=32] {'tgt'}, use_global_device_ids=true, to_apply=%region_33.34 | all-reduce | flops 2048 | bytes 16384 | tf_op jit(solution)/shard_map/psum | solution.py:55
  512.2 8.4 while.99
  520.6 39.6 %pmax.54 = f32[1024]{0:T(1024)S(1)} all-reduce(f32[1024]{0:T(1024)S(1)} %reduce_max.92), channel_id=1, replica_groups=mesh['src'=8,'tgt'=32] {'src'}, use_global_device_ids=true, to_apply=%region_39.40 | all-reduce | flops 1024 | bytes 8192 | tf_op jit(solution)/shard_map/pmax | solution.py:61
  560.3 12.4 %psum.61 = f32[1024]{0:T(1024)S(1)} all-reduce(f32[1024]{0:T(1024)S(1)} %exponential_multiply_fusion.4), channel_id=1, replica_groups=mesh['src'=8,'tgt'=32] {'src'}, use_global_device_ids=true, to_apply=%region_41.42 | all-reduce | flops 1024 | bytes 8192 | tf_op jit(solution)/shard_map/psum | solution.py:62
  573.3 8.7 while.100
  573.3 1.5 fusion.151
  575.5 1.5 fusion.151
  577.7 1.5 fusion.151
  579.9 1.5 fusion.151
  582.1 59.2 %pmax.55 = f32[2048]{0:T(1024)S(1)} all-reduce(f32[2048]{0:T(1024)S(1)} %bitcast.227), channel_id=1, replica_groups=mesh['src'=8,'tgt'=32] {'tgt'}, use_global_device_ids=true, to_apply=%region_46.47 | all-reduce | flops 2048 | bytes 16384 | tf_op jit(solution)/shard_map/pmax | solution.py:54
  641.3 57.0 %psum.62 = f32[2048]{0:T(1024)S(1)} all-reduce(f32[2048]{0:T(1024)S(1)} %exponential_multiply_fusion), channel_id=1, replica_groups=mesh['src'=8,'tgt'=32] {'tgt'}, use_global_device_ids=true, to_apply=%region_47.48 | all-reduce | flops 2048 | bytes 16384 | tf_op jit(solution)/shard_map/psum | solution.py:55
  698.9 10.4 while.101
  698.9 2.6 fusion.155
  701.5 2.6 fusion.155
  704.1 2.6 fusion.155
  706.7 2.6 fusion.155
  709.6 228.3 %reduce-scatter.2.cloned.1.call-done = f32[64,128]{1,0:T(8,128)} async-done(((f32[2048,128]{1,0:T(8,128)}), f32[64,128]{1,0:T(8,128)}) %reduce-scatter.2.cloned.1.call-update) | async-done | bytes 32784 | tf_op jit(solution)/shard_map/reduce_scatter | solution.py:114
  937.9 1.6 fusion.60
  939.5 246.2 %all-reduce.2.cloned.1.call-done = f32[128,128]{1,0:T(8,128)} async-done(((f32[128,128]{1,0:T(8,128)}), f32[128,128]{1,0:T(8,128)}) %all-reduce.2.cloned.1.call-update) | async-done | bytes 65552 | tf_op jit(solution)/shard_map/psum | solution.py:124
  1185.8 1.5 multiply_reduce_fusion
  (192 shorter events, 43.9 us)
Async XLA Ops:
  7.2 1.0 copy-start
  7.2 930.7 %reduce-scatter.2.cloned.1.call-start = ((), (), s32[]{:S(2)}) async-start(), calls=%async_computation.1 | async-start | bytes 1081344 | tf_op jit(solution)/shard_map/reduce_scatter | solution.py:114
  9.4 1.5 copy-start.1
  11.6 1.5 copy-start.1
  13.7 1.5 copy-start.1
  15.9 1.5 copy-start.1
  709.4 476.4 %all-reduce.2.cloned.1.call-start = ((), (), s32[]{:S(2)}) async-start(), calls=%async_computation.2 | async-start | bytes 131072 | tf_op jit(solution)/shard_map/psum | solution.py:124
Sparse Core Ops, SparseCore 0:
  709.5 228.3 reduce-scatter.1
  944.0 241.7 all-reduce.1
where the time goes:
time: 1200 us
  blocking collectives  628 us (52%)
  waiting for transfers between devices  475 us (40%)
  matrix products  60.8 us (5%)
  other arithmetic  18 us (2%)
  between operations  15.3 us (1%)
    psum x1, waiting for transfers between devices, shards(): covariance_sum = lax.psum(partial_value, ('src', 'tgt'))  246 us
    pmax x4, blocking collectives, across_targets(): global_peak = lax.pmax(peak_val, 'tgt')  242 us
    reduce_scatter x1, waiting for transfers between devices, shards(): lax.psum_scatter(parts_out.reshape(rows_here * lax.axis_size('tgt'), widt...  228 us
    psum x4, blocking collectives, across_targets(): totals = lax.psum(totals * jnp.exp(peak_val - global_peak), 'tgt')  228 us
    pmax x3, blocking collectives, across_sources(): global_peak = lax.pmax(peak_val, 'src')  121 us
    psum x3, blocking collectives, across_sources(): totals = lax.psum(totals * jnp.exp(peak_val - global_peak), 'src')  37.1 us
  transfers between devices with their start and end apart: 2, of which 2 were waited for; matrix products, arithmetic and copies ran while one was open for 0% of the time, Pallas kernels for 0%

commit v1 on v0

--- a/solution.py
+++ b/solution.py
@@ -121,7 +121,9 @@
     partial_value = jnp.einsum(
         "rd,re->de", source_rows.astype(jnp.float32), my_targets, precision=lax.Precision.HIGHEST
     )
-    covariance_sum = lax.psum(partial_value, ("src", "tgt"))
+    covariance_sum = partial_value
+    for name in ("tgt", "src"):
+        covariance_sum = lax.psum(covariance_sum, name)
     new_map = polar(covariance_sum)
     return (EPS * row_pot, EPS * col_pot, new_map)
 

time: 1200 us -> 1170 us (0.975)
  waiting for transfers between devices: 475 us -> 436 us
    psum x1 -> x2, waiting for transfers between devices: 246 us -> 207 us  [shards(): covariance_sum = lax.psum(covariance_sum, name)]
  transfers between devices with their start and end apart: 2 -> 3, of which waited for: 2 -> 3; matrix products, arithmetic and copies ran while one was open for 0% -> 0% of each run, Pallas kernels for 0% -> 0%
where the time goes in v1:
time: 1170 us; the launch traced here: 1160 us
  blocking collectives  628 us (54%)
  waiting for transfers between devices  436 us (37%)
  matrix products  60.8 us (5%)
  other arithmetic  18 us (2%)
  between operations  15 us (1%)
    pmax x4, blocking collectives, across_targets(): global_peak = lax.pmax(peak_val, 'tgt')  242 us
    reduce_scatter x1, waiting for transfers between devices, shards(): lax.psum_scatter(parts_out.reshape(rows_here * lax.axis_size('tgt'), widt...  228 us
    psum x4, blocking collectives, across_targets(): totals = lax.psum(totals * jnp.exp(peak_val - global_peak), 'tgt')  228 us
    psum x2, waiting for transfers between devices, shards(): covariance_sum = lax.psum(covariance_sum, name)  207 us
    pmax x3, blocking collectives, across_sources(): global_peak = lax.pmax(peak_val, 'src')  121 us
    psum x3, blocking collectives, across_sources(): totals = lax.psum(totals * jnp.exp(peak_val - global_peak), 'src')  37.1 us
    dot_general x16, matrix products, row_one_block(): jnp.einsum('rd,cd->rc', row_block, target, preferred_element_type=jnp.flo...  23.5 us
  transfers between devices with their start and end apart: 3, of which 3 were waited for; matrix products, arithmetic and copies ran while one was open for 0% of the time, Pallas kernels for 0%

profile of v1, /device:TPU:1, one launch (start us, length us, event | category | flops | bytes accessed | tf_op | source)
XLA Modules:
  0.0 1163.4 jit_solution(8729864090589498516)
XLA Ops:
  9.4 8.7 while.94
  9.4 1.5 fusion.139
  11.6 1.5 fusion.139
  13.7 1.5 fusion.139
  15.9 1.5 fusion.139
  18.1 65.3 %pmax.49 = f32[2048]{0:T(1024)S(1)} all-reduce(f32[2048]{0:T(1024)S(1)} %bitcast.221), channel_id=1, replica_groups=mesh['src'=8,'tgt'=32] {'tgt'}, use_global_device_ids=true, to_apply=%region_4.5 | all-reduce | flops 2048 | bytes 16384 | tf_op jit(solution)/shard_map/pmax | solution.py:54
  83.4 56.8 %psum.63 = f32[2048]{0:T(1024)S(1)} all-reduce(f32[2048]{0:T(1024)S(1)} %exponential_multiply_fusion.3), channel_id=1, replica_groups=mesh['src'=8,'tgt'=32] {'tgt'}, use_global_device_ids=true, to_apply=%region_5.6 | all-reduce | flops 2048 | bytes 16384 | tf_op jit(solution)/shard_map/psum | solution.py:55
  140.3 8.4 while.95
  146.6 1.4 fusion.141
  148.7 40.6 %pmax.50 = f32[1024]{0:T(1024)S(1)} all-reduce(f32[1024]{0:T(1024)S(1)} %reduce_max.90), channel_id=1, replica_groups=mesh['src'=8,'tgt'=32] {'src'}, use_global_device_ids=true, to_apply=%region_11.12 | all-reduce | flops 1024 | bytes 8192 | tf_op jit(solution)/shard_map/pmax | solution.py:61
  189.4 12.3 %psum.64 = f32[1024]{0:T(1024)S(1)} all-reduce(f32[1024]{0:T(1024)S(1)} %exponential_multiply_fusion.6), channel_id=1, replica_groups=mesh['src'=8,'tgt'=32] {'src'}, use_global_device_ids=true, to_apply=%region_13.14 | all-reduce | flops 1024 | bytes 8192 | tf_op jit(solution)/shard_map/psum | solution.py:62
  201.7 8.7 while.96
  201.7 1.5 fusion.143
  203.9 1.5 fusion.143
  206.1 1.5 fusion.143
  208.2 1.5 fusion.143
  210.4 58.5 %pmax.51 = f32[2048]{0:T(1024)S(1)} all-reduce(f32[2048]{0:T(1024)S(1)} %bitcast.223), channel_id=1, replica_groups=mesh['src'=8,'tgt'=32] {'tgt'}, use_global_device_ids=true, to_apply=%region_18.19 | all-reduce | flops 2048 | bytes 16384 | tf_op jit(solution)/shard_map/pmax | solution.py:54
  268.9 56.8 %psum.65 = f32[2048]{0:T(1024)S(1)} all-reduce(f32[2048]{0:T(1024)S(1)} %exponential_multiply_fusion.2), channel_id=1, replica_groups=mesh['src'=8,'tgt'=32] {'tgt'}, use_global_device_ids=true, to_apply=%region_19.20 | all-reduce | flops 2048 | bytes 16384 | tf_op jit(solution)/shard_map/psum | solution.py:55
  325.8 8.4 while.97
  334.2 40.5 %pmax.52 = f32[1024]{0:T(1024)S(1)} all-reduce(f32[1024]{0:T(1024)S(1)} %reduce_max.91), channel_id=1, replica_groups=mesh['src'=8,'tgt'=32] {'src'}, use_global_device_ids=true, to_apply=%region_25.26 | all-reduce | flops 1024 | bytes 8192 | tf_op jit(solution)/shard_map/pmax | solution.py:61
  374.8 12.4 %psum.66 = f32[1024]{0:T(1024)S(1)} all-reduce(f32[1024]{0:T(1024)S(1)} %exponential_multiply_fusion.5), channel_id=1, replica_groups=mesh['src'=8,'tgt'=32] {'src'}, use_global_device_ids=true, to_apply=%region_27.28 | all-reduce | flops 1024 | bytes 8192 | tf_op jit(solution)/shard_map/psum | solution.py:62
  387.2 8.7 while.98
  387.2 1.5 fusion.147
  389.4 1.5 fusion.147
  391.6 1.5 fusion.147
  393.8 1.5 fusion.147
  395.9 59.2 %pmax.53 = f32[2048]{0:T(1024)S(1)} all-reduce(f32[2048]{0:T(1024)S(1)} %bitcast.225), channel_id=1, replica_groups=mesh['src'=8,'tgt'=32] {'tgt'}, use_global_device_ids=true, to_apply=%region_32.33 | all-reduce | flops 2048 | bytes 16384 | tf_op jit(solution)/shard_map/pmax | solution.py:54
  455.1 57.0 %psum.67 = f32[2048]{0:T(1024)S(1)} all-reduce(f32[2048]{0:T(1024)S(1)} %exponential_multiply_fusion.1), channel_id=1, replica_groups=mesh['src'=8,'tgt'=32] {'tgt'}, use_global_device_ids=true, to_apply=%region_33.34 | all-reduce | flops 2048 | bytes 16384 | tf_op jit(solution)/shard_map/psum | solution.py:55
  512.2 8.4 while.99
  520.6 39.6 %pmax.54 = f32[1024]{0:T(1024)S(1)} all-reduce(f32[1024]{0:T(1024)S(1)} %reduce_max.92), channel_id=1, replica_groups=mesh['src'=8,'tgt'=32] {'src'}, use_global_device_ids=true, to_apply=%region_39.40 | all-reduce | flops 1024 | bytes 8192 | tf_op jit(solution)/shard_map/pmax | solution.py:61
  560.3 12.4 %psum.68 = f32[1024]{0:T(1024)S(1)} all-reduce(f32[1024]{0:T(1024)S(1)} %exponential_multiply_fusion.4), channel_id=1, replica_groups=mesh['src'=8,'tgt'=32] {'src'}, use_global_device_ids=true, to_apply=%region_41.42 | all-reduce | flops 1024 | bytes 8192 | tf_op jit(solution)/shard_map/psum | solution.py:62
  573.3 8.7 while.100
  573.3 1.5 fusion.151
  575.5 1.5 fusion.151
  577.7 1.5 fusion.151
  579.9 1.5 fusion.151
  582.1 59.2 %pmax.55 = f32[2048]{0:T(1024)S(1)} all-reduce(f32[2048]{0:T(1024)S(1)} %bitcast.227), channel_id=1, replica_groups=mesh['src'=8,'tgt'=32] {'tgt'}, use_global_device_ids=true, to_apply=%region_46.47 | all-reduce | flops 2048 | bytes 16384 | tf_op jit(solution)/shard_map/pmax | solution.py:54
  641.3 57.0 %psum.69 = f32[2048]{0:T(1024)S(1)} all-reduce(f32[2048]{0:T(1024)S(1)} %exponential_multiply_fusion), channel_id=1, replica_groups=mesh['src'=8,'tgt'=32] {'tgt'}, use_global_device_ids=true, to_apply=%region_47.48 | all-reduce | flops 2048 | bytes 16384 | tf_op jit(solution)/shard_map/psum | solution.py:55
  698.9 10.4 while.101
  698.9 2.6 fusion.155
  701.5 2.6 fusion.155
  704.1 2.6 fusion.155
  706.7 2.6 fusion.155
  709.4 228.5 %reduce-scatter.2.cloned.1.call-done = f32[64,128]{1,0:T(8,128)} async-done(((f32[2048,128]{1,0:T(8,128)}), f32[64,128]{1,0:T(8,128)}) %reduce-scatter.2.cloned.1.call-update) | async-done | bytes 32784 | tf_op jit(solution)/shard_map/reduce_scatter | solution.py:114
  937.9 1.6 fusion.60
  939.8 140.9 %all-reduce.3.cloned.1.call-done = f32[128,128]{1,0:T(8,128)} async-done(((f32[128,128]{1,0:T(8,128)}), f32[128,128]{1,0:T(8,128)}) %all-reduce.3.cloned.1.call-update) | async-done | bytes 65552 | tf_op jit(solution)/shard_map/psum | solution.py:126
  1080.7 66.4 %all-reduce.5.cloned.1.call-done = f32[128,128]{1,0:T(8,128)} async-done(((f32[128,128]{1,0:T(8,128)}), f32[128,128]{1,0:T(8,128)}) %all-reduce.5.cloned.1.call-update) | async-done | bytes 65552 | tf_op jit(solution)/shard_map/psum | solution.py:126
  1147.2 1.5 multiply_reduce_fusion
  (195 shorter events, 45.3 us)
Async XLA Ops:
  7.2 1.0 copy-start
  7.2 930.7 %reduce-scatter.2.cloned.1.call-start = ((), (), s32[]{:S(2)}) async-start(), calls=%async_computation.1 | async-start | bytes 1081344 | tf_op jit(solution)/shard_map/reduce_scatter | solution.py:114
  9.4 1.5 copy-start.1
  11.6 1.5 copy-start.1
  13.7 1.5 copy-start.1
  15.9 1.5 copy-start.1
  709.4 371.3 %all-reduce.3.cloned.1.call-start = ((), (), s32[]{:S(2)}) async-start(), calls=%async_computation.2 | async-start | bytes 131072 | tf_op jit(solution)/shard_map/psum | solution.py:126
  939.5 207.6 %all-reduce.5.cloned.1.call-start = ((), (), s32[]{:S(2)}) async-start(), calls=%async_computation.3 | async-start | bytes 131072 | tf_op jit(solution)/shard_map/psum | solution.py:126
Sparse Core Ops, SparseCore 0:
  709.5 228.3 reduce-scatter.1
  941.9 138.7 all-reduce.2
  1083.0 64.0 all-reduce.4
